TPU v7x, 512 devices: a whole 4x8x8 slice. The times are simulated.
512 devices in a mesh: layer: 2 (over z_hi), row: 16 (over z_lo, x), col: 16 (over y, core).
Axes of the slice: x: 4, y: 8, z: 8 (z_hi: 2, z_lo: 4; z = z_hi * 4 + z_lo), core: 2. Of those that a mesh axis runs over, the one named last changes fastest.
Arguments:
- trail: bfloat16 [16384, 2, 16384], P('row', 'layer', 'col'), may hold values from -6 to 6
- lower_panels: bfloat16 [2, 2, 256, 16384], P('layer', None, 'col', 'row'), may hold values from -6 to 6
- upper_panels: bfloat16 [2, 2, 256, 2, 16384], P('layer', None, 'row', None, 'col'), may hold values from -0.375 to 0.375
- lower_inverse: bfloat16 [2, 2, 256, 256], P('layer'), may hold values from -0.375 to 0.375
- upper_inverse: bfloat16 [2, 2, 256, 256], P('layer'), may hold values from -0.375 to 0.375
- above_block: bfloat16 [2, 256, 256], P('layer'), may hold values from -0.375 to 0.375
- left_block: bfloat16 [2, 256, 256], P('layer'), may hold values from -0.375 to 0.375
- row_order: int32 [2, 2, 256], P('layer'), may hold values from 0 to 255, each once within a row
- row_mask: int32 [2, 2, 64], P('layer', None, 'row'), may hold values 0 or 1
- column_mask: int32 [2, 2, 2, 64], P('layer', None, None, 'col'), may hold values 0 or 1
Outputs:
- updated: bfloat16 [16384, 2, 16384], P('row', 'layer', 'col')
Inputs may be any that keep to these rules, and one draw needn't show every extreme that they name: Each row_order[l,k] is a permutation of 0 to 255.
All inputs are finite; a program needn't handle non-finite values. No bound on the sum of `row_mask` or of `column_mask` on one device may be relied on, other than what follows from the above.
Results may differ from a plain program's by a relative error of at most 0.012.
Values may be sent and summed in bfloat16 or wider, within the bound.
A program may use at most 64 MiB of HBM per device.

v0:
```python
import jax
import jax.numpy as jnp
from jax import lax
from jax.sharding import PartitionSpec as P


def build_factors(cols_all, rows_flat, low_inv, up_inv, above, left, order, lmask, umask):
    nb = cols_all.shape[1]
    rows_scale = jnp.repeat(lmask.astype(jnp.float32), nb, axis=1)
    cols_scale = jnp.repeat(umask.astype(jnp.float32), nb, axis=2).reshape(2, -1)
    upper_first = (
        jnp.dot(
            low_inv[0], jnp.take(rows_flat[0], order[0], axis=0), preferred_element_type=jnp.float32
        )
        * cols_scale[0]
    ).astype(jnp.bfloat16)
    lower_first = (
        lax.dot_general(
            cols_all[0], up_inv[0], (((0,), (0,)), ((), ())), preferred_element_type=jnp.float32
        )
        * rows_scale[0][:, None]
    ).astype(jnp.bfloat16)
    upper_cross = jnp.dot(
        low_inv[0], jnp.take(above, order[0], axis=0), preferred_element_type=jnp.float32
    ).astype(jnp.bfloat16)
    lower_cross = jnp.dot(left, up_inv[0], preferred_element_type=jnp.float32).astype(jnp.bfloat16)
    column_next = (
        cols_all[1].T.astype(jnp.float32)
        - jnp.dot(lower_first, upper_cross, preferred_element_type=jnp.float32)
    ).astype(jnp.bfloat16)
    row_next = (
        rows_flat[1].astype(jnp.float32)
        - jnp.dot(lower_cross, upper_first, preferred_element_type=jnp.float32)
    ).astype(jnp.bfloat16)
    upper_second = (
        jnp.dot(
            low_inv[1], jnp.take(row_next, order[1], axis=0), preferred_element_type=jnp.float32
        )
        * cols_scale[1]
    ).astype(jnp.bfloat16)
    lower_second = (
        jnp.dot(column_next, up_inv[1], preferred_element_type=jnp.float32) * rows_scale[1][:, None]
    ).astype(jnp.bfloat16)
    return (lower_first, upper_first, lower_second, upper_second)


def on_device(
    trail,
    lower_panels,
    upper_panels,
    lower_inverse,
    upper_inverse,
    above_block,
    left_block,
    row_order,
    row_mask,
    column_mask,
):
    cols_all = lax.all_gather(lower_panels, "col", axis=2, tiled=True)[0]
    rows_all = lax.all_gather(upper_panels, "row", axis=2, tiled=True)[0]
    panel_width = rows_all.shape[1]
    half_width = rows_all.shape[3]
    rows_flat = rows_all.reshape(2, panel_width, 2 * half_width)
    lower_first, upper_first, lower_second, upper_second = build_factors(
        cols_all,
        rows_flat,
        lower_inverse[0],
        upper_inverse[0],
        above_block[0],
        left_block[0],
        row_order[0],
        row_mask[0],
        column_mask[0],
    )
    local_rows = lower_first.shape[0]
    partial_value = -(
        jnp.dot(lower_first, upper_first, preferred_element_type=jnp.float32)
        + jnp.dot(lower_second, upper_second, preferred_element_type=jnp.float32)
    )
    partial_value = partial_value.reshape(local_rows, 2, half_width)
    summed = lax.psum_scatter(
        partial_value.astype(jnp.bfloat16), "layer", scatter_dimension=1, tiled=True
    ).astype(jnp.float32)
    return (trail.astype(jnp.float32) + summed).astype(jnp.bfloat16)


def solution(mesh):
    placed = (
        P("row", "layer", "col"),
        P("layer", None, "col", "row"),
        P("layer", None, "row", None, "col"),
        P("layer", None, None, None),
        P("layer", None, None, None),
        P("layer", None, None),
        P("layer", None, None),
        P("layer", None, None),
        P("layer", None, "row"),
        P("layer", None, None, "col"),
    )
    return jax.shard_map(
        on_device, mesh=mesh, in_specs=placed, out_specs=P("row", "layer", "col"), check_vma=False
    )
```

profile of v0, /device:TPU:1, one launch (start us, length us, event | category | flops | bytes accessed | tf_op | source)
XLA Modules:
  0.0 291.8 jit_solution(12214837924002246565)
XLA Ops:
  6.5 0.7 all-gather.3.cloned.1.call-update
  7.3 0.0 all-gather.5.cloned.1.call-start
  7.3 0.7 all-gather.5.cloned.1.call-update
  8.0 0.0 reduce-scatter.2.cloned.1.call-start
  8.1 0.7 convert_element_type.66
  8.7 0.7 convert_element_type.68
  9.4 0.1 broadcast_bitcast_fusion.2
  9.5 0.1 broadcast_bitcast_fusion
  9.6 0.7 compare_select_fusion
  10.3 1.9 gather_fusion
  12.2 0.8 fusion.41
  13.0 0.6 pad_clamp_fusion
  13.6 0.6 pad_clamp_fusion.2
  14.2 0.6 compare_and_fusion
  14.8 1.2 convolution_convert_fusion.1
  16.0 40.3 %all-gather.3.cloned.1.call-done = bf16[1,2,256,1024]{3,2,1,0:T(8,128)(2,1)} async-done(((bf16[1,2,16,1024]{3,2,1,0:T(8,128)(2,1)}), bf16[1,2,256,1024]{3,2,1,0:T(8,128)(2,1)}) %all-gather.3.cloned.1.call-update) | async-done | bytes 1048592 | tf_op jit(solution)/shard_map/all_gather | solution.py:59
  56.3 1.4 fusion.3
  57.7 2.7 fusion.5
  60.5 73.3 %all-gather.5.cloned.1.call-done = bf16[1,2,256,2,1024]{4,3,2,1,0:T(2,128)(2,1)} async-done(((bf16[1,2,16,2,1024]{4,3,2,1,0:T(2,128)(2,1)}), bf16[1,2,256,2,1024]{4,3,2,1,0:T(2,128)(2,1)}) %all-gather.5.cloned.1.call-update) | async-done | bytes 2097168 | tf_op jit(solution)/shard_map/all_gather | solution.py:60
  133.8 2.7 slice_convert_fusion
  136.5 0.9 copy.18
  137.4 0.3 copy.15
  137.7 2.6 gather_fusion.1
  140.3 2.0 fusion
  142.3 4.5 %fusion.42 = f32[1024,2048]{1,0:T(8,128)} fusion(bf16[1024,256]{1,0:T(8,128)(2,1)S(1)} %copy-done.4, bf16[2048,256]{1,0:T(8,128)(2,1)S(1)} %fusion), kind=kOutput, calls=%fused_computation.67 | convolution fusion | flops 1073741824 | bytes 9961472 | tf_op jit(solution)/shard_map/dot_general | solution.py:77
  146.9 1.9 fusion.1
  148.8 1.6 gather_fusion.2
  150.4 6.0 %negate_convert_fusion = bf16[1024,2048]{1,0:T(8,128)(2,1)} fusion(f32[1024,2048]{1,0:T(8,128)} %fusion.42, bf16[1024,256]{1,0:T(8,128)(2,1)S(1)} %copy-done.5, bf16[256,2048]{1,0:T(8,128)(2,1)S(1)} %gather_fusion.2, f32[2048]{0:T(1024)S(1)} %bitcast.85, pred[256]{0:T(512)(128)(4,1)S(1)} %copy-done.8, bf16[1,2,256,256]{3,2,1,0:T(8,128)(2,1)S(1)} %copy-done.6), kind=kOutput, calls=%fused_computation.3 | convolution fusion | flops 1350041600 | bytes 14295552 | tf_op jit(solution)/shard_map/dot_general | solution.py:78
  156.4 4.7 %copy.21 = bf16[128,2,8,1024]{3,2,0,1:T(8,128)(2,1)} copy(bf16[128,2,8,1024]{3,2,1,0:T(8,128)(2,1)} %bitcast.80) | data formatting | bytes 8388608 | tf_op jit(solution)/shard_map/convert_element_type | solution.py:82
  161.0 0.0 reduce-scatter.2.cloned.1.call-update
  161.1 120.3 %reduce-scatter.2.cloned.1.call-done = bf16[1024,1,1024]{2,0,1:T(8,128)(2,1)} async-done(((bf16[1024,2,1024]{2,0,1:T(8,128)(2,1)}), bf16[1024,1,1024]{2,0,1:T(8,128)(2,1)}) %reduce-scatter.2.cloned.1.call-update) | async-done | bytes 2097168 | tf_op jit(solution)/shard_map/reduce_scatter | solution.py:81
  281.4 3.9 %add_convert_fusion = bf16[1024,1,1024]{2,0,1:T(8,128)(2,1)} fusion(bf16[1024,1,1024]{2,0,1:T(8,128)(2,1)} %reduce-scatter.2.cloned.1.call-done, bf16[1024,1,1024]{2,0,1:T(8,128)(2,1)S(1)} %copy-done.2), kind=kLoop, calls=%fused_computation.5 | loop fusion | flops 4194304 | bytes 6291456 | tf_op jit(solution)/shard_map/convert_element_type | solution.py:84
  (31 shorter events, 0.1 us)
Async XLA Ops:
  6.5 140.3 %copy-start = (bf16[1,256,256]{2,1,0:T(8,128)(2,1)S(1)}, bf16[1,256,256]{2,1,0:T(8,128)(2,1)}, u32[]{:S(2)}) copy-start(bf16[1,256,256]{2,1,0:T(8,128)(2,1)} %param.18) | copy-start | bytes 393220
  6.5 51.2 %copy-start.7 = (bf16[1,2,256,256]{3,2,1,0:T(8,128)(2,1)S(1)}, bf16[1,2,256,256]{3,2,1,0:T(8,128)(2,1)}, u32[]{:S(2)}) copy-start(bf16[1,2,256,256]{3,2,1,0:T(8,128)(2,1)} %param.16) | copy-start | bytes 786436
  6.5 49.7 %all-gather.3.cloned.1.call-start = ((), (), s32[]{:S(2)}) async-start(), calls=%async_computation.1 | async-start | bytes 1114112 | tf_op jit(solution)/shard_map/all_gather | solution.py:59
  7.3 126.6 %all-gather.5.cloned.1.call-start = ((), (), s32[]{:S(2)}) async-start(), calls=%async_computation.2 | async-start | bytes 2228224 | tf_op jit(solution)/shard_map/all_gather | solution.py:60
  8.0 273.4 %reduce-scatter.2.cloned.1.call-start = ((), (), s32[]{:S(2)}) async-start(), calls=%async_computation.3 | async-start | bytes 6291456 | tf_op jit(solution)/shard_map/reduce_scatter | solution.py:81
  14.2 46.3 %copy-start.9 = (pred[256]{0:T(512)(128)(4,1)}, pred[256]{0:T(512)(128)(4,1)S(1)}, u32[]{:S(2)}) copy-start(pred[256]{0:T(512)(128)(4,1)S(1)} %compare_and_fusion.1) | copy-start | bytes 772
  57.7 78.8 %copy-start.3 = (bf16[1024,256]{1,0:T(8,128)(2,1)}, bf16[1024,256]{1,0:T(8,128)(2,1)S(1)}, u32[]{:S(2)}) copy-start(bf16[1024,256]{1,0:T(8,128)(2,1)S(1)} %fusion.3) | copy-start | bytes 1572868
  137.7 2.6 copy-start.6
  140.3 2.0 copy-start.4
  142.3 4.6 %copy-start.1 = (bf16[2048,256]{1,0:T(8,128)(2,1)}, bf16[2048,256]{1,0:T(8,128)(2,1)S(1)}, u32[]{:S(2)}) copy-start(bf16[2048,256]{1,0:T(8,128)(2,1)S(1)} %fusion) | copy-start | bytes 3145732
  148.8 1.7 copy-start.5
  148.8 1.7 copy-start.8
  161.0 120.3 %copy-start.2 = (bf16[1024,1,1024]{2,0,1:T(8,128)(2,1)S(1)}, bf16[1024,1,1024]{2,0,1:T(8,128)(2,1)}, u32[]{:S(2)}) copy-start(bf16[1024,1,1024]{2,0,1:T(8,128)(2,1)} %param.12) | copy-start | bytes 6291460
Sparse Core Ops, SparseCore 0:
  9.5 46.7 all-gather.2
  58.4 75.4 all-gather.4
  161.2 120.1 reduce-scatter.1
where the time goes:
time: 292 us
  waiting for transfers between devices  235 us (80%)
  matrix products  19.8 us (7%)
  between operations  13.3 us (5%)
  local copies, waits for them, and re-layouts  12.9 us (4%)
  other arithmetic  10.4 us (4%)
    reduce_scatter x1, waiting for transfers between devices, on_device(): lax.psum_scatter(partial_value.astype(jnp.bfloat16), 'layer', scatter_dim...  120 us
    all_gather x1, waiting for transfers between devices, on_device(): rows_all = lax.all_gather(upper_panels, 'row', axis=2, tiled=True)[0]  73.3 us
    all_gather x1, waiting for transfers between devices, on_device(): cols_all = lax.all_gather(lower_panels, 'col', axis=2, tiled=True)[0]  40.3 us
    dot_general x1, matrix products, on_device(): jnp.dot(lower_second, upper_second, preferred_element_type=jnp.float32)  5.95 us
  transfers between devices with their start and end apart: 3, of which 3 were waited for; matrix products, arithmetic and copies ran while one was open for 4% of the time, Pallas kernels for 0%

commit v1 on v0

v1 whole, which is shorter than its diff:
```python
import functools

import jax
import jax.numpy as jnp
from jax import lax
from jax.experimental import pallas as pl
from jax.experimental.pallas import tpu as pltpu
from jax.sharding import PartitionSpec as P

NZ, NX, NY = 4, 4, 8
NB = 256
SUB = 16
W = 1024
PANEL = 2 * W
CROSS = PANEL + 6 * NB
M0, M1, V, UI0, UI1, WW = (PANEL + i * NB for i in range(6))
F32, BF16 = jnp.float32, jnp.bfloat16


def dot(a, b):
    return jnp.dot(a, b, preferred_element_type=F32)


def dot_tn(a, b):
    return lax.dot_general(a, b, (((0,), (0,)), ((), ())), preferred_element_type=F32)


def dot_nt(a, b):
    return lax.dot_general(a, b, (((1,), (1,)), ((), ())), preferred_element_type=F32)


def kernel(
    trail_ref, lp_ref, uh_ref, li_ref, ui_ref, above_ref, left_ref, order_ref, rmask_ref, cmask_ref,
    out_ref,
    lo, xb, stage, uo, uc, own, masks, xmasks, lf, uf, acc, trail_v, out_v,
    send, recv, local,
):
    layer = lax.axis_index("layer")
    row = lax.axis_index("row")
    col = lax.axis_index("col")
    zl, x, y, core = row // NX, row % NX, col // 2, col % 2

    def at(dl=0, dz=0, dx=0, dy=0, dc=0):
        return (
            (layer + dl) % 2,
            (zl + dz + NZ) % NZ * NX + (x + dx + NX) % NX,
            (y + dy + NY) % NY * 2 + (core + dc) % 2,
        )

    def lslot(dy, dc=0):
        return pl.ds(pl.multiple_of(((y + dy + NY) % NY * 2 + (core + dc) % 2) * SUB, SUB), SUB)

    def uslot(dz, dx):
        return pl.ds(
            pl.multiple_of(((zl + dz + NZ) % NZ * NX + (x + dx + NX) % NX) * SUB, SUB), SUB
        )

    barrier = pltpu.get_barrier_semaphore()
    peers = [dict(dy=1), dict(dy=-1), dict(dx=1), dict(dx=-1), dict(dz=1), dict(dz=2), dict(dz=3),
             dict(dl=1), dict(dc=1)]
    for p in peers:
        pl.semaphore_signal(barrier, 1, device_id=at(**p), device_id_type=pl.DeviceIdType.MESH)

    fetch = pltpu.make_async_copy(trail_ref, trail_v, local.at[0])
    fetch.start()

    for k in range(2):
        stage[:, pl.ds(k * W, W)] = lp_ref[k]
    lo[lslot(0)] = stage[:, :PANEL]
    uo[uslot(0, 0)] = uh_ref[layer]
    masks[...] = jnp.zeros_like(masks)
    masks[0:2, 0:4] = rmask_ref[...].astype(F32)
    for k in range(2):
        for h in range(2):
            r = 2 + 2 * h + k
            masks[r : r + 1, 0:4] = cmask_ref[k, h : h + 1, :].astype(F32)

    place = lax.broadcasted_iota(jnp.int32, (NB, NB), 0)

    def permuted(rows, k):
        hot = jnp.where(place == order_ref[k : k + 1, :], 1.0, 0.0).astype(BF16)
        return dot_nt(rows, hot).astype(BF16)

    share = lslot(0)
    m0 = permuted(li_ref[0, share], 0)
    m1 = permuted(li_ref[1, share], 1)
    lower_cross = dot(left_ref[...], ui_ref[0]).astype(BF16)
    upper_cross = dot(m0, above_ref[...]).astype(BF16)
    for place_at, value in (
        (M0, m0),
        (M1, m1),
        (V, dot(m1, lower_cross).astype(BF16)),
        (UI0, ui_ref[0, share]),
        (UI1, ui_ref[1, share]),
        (WW, dot(upper_cross, ui_ref[1]).astype(BF16)),
    ):
        stage[:, pl.ds(place_at, NB)] = value

    pl.semaphore_wait(barrier, len(peers))

    used = [0]
    started = []

    def new(src, dst, to):
        i = used[0]
        used[0] += 1
        return pltpu.make_async_remote_copy(
            src_ref=src, dst_ref=dst, send_sem=send.at[i], recv_sem=recv.at[i],
            device_id=at(**to), device_id_type=pl.DeviceIdType.MESH,
        )

    def go(ref, to, dst=None):
        copy = new(ref, ref if dst is None else dst, to)
        copy.start()
        started.append(copy)
        return copy

    cx = go(stage, dict(dl=1), xb.at[share])
    cu = go(uh_ref.at[1 - layer], dict(dl=1), uc.at[uslot(0, 0)])
    cm = go(masks, dict(dl=1), xmasks)

    class Ring:
        def __init__(self, buf, width):
            self.buf, self.width, self.half = buf, width, width // 2
            self.sib = []

        def slot(self, dy, part=None):
            if part is None:
                return self.buf.at[lslot(dy)]
            return self.buf.at[lslot(dy), pl.ds(part * self.half, self.half)]

        def begin(self):
            self.up = go(self.slot(0), dict(dy=1))
            self.down = go(self.slot(0), dict(dy=-1))
            self.sib.append(go(self.slot(0), dict(dc=1)))

        def step(self, s):
            self.up.wait_recv()
            if s < 3:
                nup = go(self.slot(-s), dict(dy=1))
            elif s == 3:
                nup = go(self.slot(-3, 0), dict(dy=1))
            self.down.wait_recv()
            if s < 3:
                ndown = go(self.slot(s), dict(dy=-1))
            elif s == 3:
                ndown = go(self.slot(3, 1), dict(dy=-1))
            if s < 4:
                self.sib.append(go(self.slot(-s), dict(dc=1)))
                self.sib.append(go(self.slot(s), dict(dc=1)))
                self.up, self.down = nup, ndown
            else:
                self.sib.append(go(self.slot(4), dict(dc=1)))

        def end(self):
            for c in self.sib:
                c.wait_recv()

    class Plane:
        def __init__(self, buf):
            self.buf = buf
            self.z, self.p, self.m, self.f, self.g = {}, {}, {}, {}, {}

        def slot(self, dz, dx, part=None):
            if part is None:
                return self.buf.at[uslot(dz, dx)]
            return self.buf.at[uslot(dz, dx), pl.ds(part * W, W)]

        def begin(self):
            self.p[0] = go(self.slot(0, 0), dict(dx=1))
            self.m[0] = go(self.slot(0, 0), dict(dx=-1))
            for d in (1, 3, 2):
                self.z[d] = go(self.slot(0, 0), dict(dz=d))

        def spread(self, d):
            self.z[d].wait_recv()
            self.p[d] = go(self.slot(-d, 0), dict(dx=1))
            self.m[d] = go(self.slot(-d, 0), dict(dx=-1))

        def forward(self, d):
            self.p[d].wait_recv()
            self.f[d] = go(self.slot(-d, -1, 0), dict(dx=1))
            self.m[d].wait_recv()
            self.g[d] = go(self.slot(-d, 1, 1), dict(dx=-1))

        def end(self):
            for d in range(4):
                self.f[d].wait_recv()
                self.g[d].wait_recv()

    ring0, ring1 = Ring(lo, PANEL), Ring(xb, CROSS)
    plane0, plane1 = Plane(uo), Plane(uc)

    def lower_factors(i, buf, ui0, ui1, w, mask):
        for b in range(4):
            rows = pl.ds(b * NB, NB)
            first = (dot_tn(buf[:, pl.ds(b * NB, NB)], ui0) * mask[0:1, b : b + 1]).astype(BF16)
            second = dot_tn(buf[:, pl.ds(W + b * NB, NB)], ui1) - dot(first, w)
            lf[i, rows, 0:NB] = first
            lf[i, rows, NB : 2 * NB] = (second * mask[1:2, b : b + 1]).astype(BF16)

    def upper_factors(i, buf, m0, m1, v, mask):
        c0 = mask[pl.ds(2 + 2 * layer, 1), :]
        c1 = mask[pl.ds(3 + 2 * layer, 1), :]
        for b in range(4):
            cols = pl.ds(b * NB, NB)
            first = (dot(m0, buf[:, cols]) * c0[:, b : b + 1]).astype(BF16)
            second = dot(m1, buf[:, pl.ds(W + b * NB, NB)]) - dot(v, first)
            uf[i, 0:NB, cols] = first
            uf[i, NB : 2 * NB, cols] = (second * c1[:, b : b + 1]).astype(BF16)

    def product(i, b):
        return dot(lf[i, pl.ds(b * NB, NB)], uf[i])

    ring0.begin()
    plane0.begin()
    own[0] = permuted(li_ref[0], 0)
    own[1] = permuted(li_ref[1], 1)
    own[2] = dot(own[1], lower_cross).astype(BF16)
    own[3] = dot(dot(own[0], above_ref[...]).astype(BF16), ui_ref[1]).astype(BF16)

    ring0.step(1)
    plane0.forward(0)
    plane0.spread(1)
    plane0.spread(3)
    plane0.spread(2)
    ring0.step(2)
    cu.wait_recv()
    plane1.begin()
    cx.wait_recv()
    ring1.begin()
    ring0.step(3)
    plane0.forward(1)
    plane0.forward(3)
    ring1.step(1)
    plane1.forward(0)
    plane0.forward(2)
    ring0.step(4)
    ring0.end()
    ring1.step(2)
    plane1.spread(1)
    plane1.spread(3)
    plane1.spread(2)
    lower_factors(0, lo, ui_ref[0], ui_ref[1], own[3], masks)
    ring1.step(3)
    plane1.forward(1)
    plane1.forward(3)
    plane1.forward(2)
    plane0.end()
    upper_factors(0, uo, own[0], own[1], own[2], masks)
    ring1.step(4)

    @pl.loop(0, 4)
    def _(b):
        acc[pl.ds(pl.multiple_of(b * NB, NB), NB)] = product(0, b)

    ring1.end()
    cm.wait_recv()
    lower_factors(
        1, xb, xb[:, pl.ds(UI0, NB)], xb[:, pl.ds(UI1, NB)], xb[:, pl.ds(WW, NB)], xmasks
    )
    plane1.end()
    upper_factors(1, uc, xb[:, pl.ds(M0, NB)], xb[:, pl.ds(M1, NB)], xb[:, pl.ds(V, NB)], xmasks)
    fetch.wait()

    @pl.loop(0, 4)
    def _(b):
        rows = pl.ds(pl.multiple_of(b * NB, NB), NB)
        total = acc[rows] + product(1, b)
        out_v[rows] = (trail_v[rows].astype(F32) - total).astype(BF16)

    put = pltpu.make_async_copy(out_v, out_ref, local.at[1])
    put.start()
    for c in started:
        c.wait_send()
    put.wait()


def on_device(trail, lower, upper, li, ui, above, left, order, rmask, cmask):
    halves = jnp.transpose(upper[0], (2, 1, 0, 3)).reshape(2, SUB, PANEL)
    vmem = pl.BlockSpec(memory_space=pltpu.VMEM)
    hbm = pl.BlockSpec(memory_space=pl.ANY)
    n = 96
    out = pl.pallas_call(
        kernel,
        out_shape=jax.ShapeDtypeStruct((W, W), BF16),
        in_specs=[hbm] + [vmem] * 9,
        out_specs=hbm,
        scratch_shapes=[
            pltpu.VMEM((NB, PANEL), BF16),
            pltpu.VMEM((NB, CROSS), BF16),
            pltpu.VMEM((SUB, CROSS), BF16),
            pltpu.VMEM((NB, PANEL), BF16),
            pltpu.VMEM((NB, PANEL), BF16),
            pltpu.VMEM((4, NB, NB), BF16),
            pltpu.VMEM((8, 128), F32),
            pltpu.VMEM((8, 128), F32),
            pltpu.VMEM((2, W, 2 * NB), BF16),
            pltpu.VMEM((2, 2 * NB, W), BF16),
            pltpu.VMEM((W, W), F32),
            pltpu.VMEM((W, W), BF16),
            pltpu.VMEM((W, W), BF16),
            pltpu.SemaphoreType.DMA((n,)),
            pltpu.SemaphoreType.DMA((n,)),
            pltpu.SemaphoreType.DMA((2,)),
        ],
        compiler_params=pltpu.CompilerParams(
            collective_id=0, has_side_effects=True, vmem_limit_bytes=48 * 2**20
        ),
        name="panels_update",
    )(trail[:, 0, :], lower[0], halves, li[0], ui[0], above[0], left[0], order[0], rmask[0], cmask[0])
    return out[:, None, :]


def solution(mesh):
    placed = (
        P("row", "layer", "col"),
        P("layer", None, "col", "row"),
        P("layer", None, "row", None, "col"),
        P("layer", None, None, None),
        P("layer", None, None, None),
        P("layer", None, None),
        P("layer", None, None),
        P("layer", None, None),
        P("layer", None, "row"),
        P("layer", None, None, "col"),
    )
    return jax.shard_map(
        on_device, mesh=mesh, in_specs=placed, out_specs=P("row", "layer", "col"), check_vma=False
    )
```

time: 292 us -> 66 us (0.23)
  waiting for transfers between devices: 235 us -> 0 us
  Pallas kernels: 0 us -> 55 us
  matrix products: 19.8 us -> 0 us
  between operations: 13.3 us -> 0.03 us
  other arithmetic: 10.4 us -> 0 us
    reduce_scatter x1 -> x0, waiting for transfers between devices: 120 us -> none  [on_device(): lax.psum_scatter(partial_value.astype(jnp.bfloat16), 'layer', scatter_dim...]
    all_gather x2 -> x0, waiting for transfers between devices: 114 us -> none  [the longest x1 73.3 us: on_device(): rows_all = lax.all_gather(upper_panels, 'row', axis=2, tiled=True)[0]]
    pallas_call x0 -> x1, Pallas kernels: none -> 55 us  [on_device(): pl.pallas_call(kernel, out_shape=jax.ShapeDtypeStruct((W, W), BF16), in_s...]
    dot_general x7 -> x0, matrix products: 19.8 us -> none  [the longest x1 5.95 us: on_device(): jnp.dot(lower_second, upper_second, preferred_element_type=jnp.float32)]
    unnamed x28 -> x19, local copies, waits for them, and re-layouts: 1.35 us -> 9.49 us
    convert_element_type x4 -> x0, other arithmetic: 7.91 us -> none  [the longest x1 3.87 us: on_device(): return (trail.astype(jnp.float32) + summed).astype(jnp.bfloat16)]
    gather x3 -> x0, local copies, waits for them, and re-layouts: 6.11 us -> none  [the longest x1 2.6 us: build_factors(): jnp.take(rows_flat[0], order[0], axis=0)]
    convert_element_type x1 -> x0, local copies, waits for them, and re-layouts: 4.67 us -> none  [on_device(): partial_value.astype(jnp.bfloat16)]
  transfers between devices with their start and end apart: 3 -> 0, of which waited for: 3 -> 0; matrix products, arithmetic and copies ran while one was open for 4% -> 0% of each run, Pallas kernels for 0% -> 0%
where the time goes in v1:
time: 66 us; the launch traced here: 65.7 us
  Pallas kernels  55 us (83%)
  local copies, waits for them, and re-layouts  10.6 us (16%)
    pallas_call x1, Pallas kernels, on_device(): pl.pallas_call(kernel, out_shape=jax.ShapeDtypeStruct((W, W), BF16), in_s...  55 us
    unnamed x19, local copies, waits for them, and re-layouts  9.49 us

profile of v1, /device:TPU:1, one launch (start us, length us, event | category | flops | bytes accessed | tf_op | source)
XLA Modules:
  0.0 65.7 jit_solution(1431222792999357482)
XLA Ops:
  0.0 1.0 %copy.11 = bf16[2,16,2,1024]{3,2,1,0:T(2,128)(2,1)S(1)} copy(bf16[2,16,2,1024]{3,0,1,2:T(2,128)(2,1)} %bitcast.23) | data formatting | bytes 262144 | tf_op jit(solution)/shard_map/transpose | solution.py:280
  1.0 0.1 reshape.3.uh_ref
  1.1 0.0 copy-start
  1.1 1.6 %copy-done = bf16[1024,1,1024]{2,0,1:T(8,128)(2,1)S(1)} copy-done((bf16[1024,1,1024]{2,0,1:T(8,128)(2,1)S(1)}, bf16[1024,1,1024]{2,0,1:T(8,128)(2,1)}, u32[]{:S(2)}) %copy-start) | copy-done | bytes 2097176
  2.7 0.0 copy-start.1
  2.7 0.9 %copy-done.1 = bf16[1,2,256,256]{3,2,1,0:T(8,128)(2,1)S(1)} copy-done((bf16[1,2,256,256]{3,2,1,0:T(8,128)(2,1)S(1)}, bf16[1,2,256,256]{3,2,1,0:T(8,128)(2,1)}, u32[]{:S(2)}) %copy-start.1) | copy-done | bytes 262168
  3.7 0.0 copy-start.2
  3.7 0.9 %copy-done.2 = bf16[1,2,256,256]{3,2,1,0:T(8,128)(2,1)S(1)} copy-done((bf16[1,2,256,256]{3,2,1,0:T(8,128)(2,1)S(1)}, bf16[1,2,256,256]{3,2,1,0:T(8,128)(2,1)}, u32[]{:S(2)}) %copy-start.2) | copy-done | bytes 262168
  4.6 0.0 copy-start.3
  4.6 0.9 %copy-done.3 = bf16[1,256,256]{2,1,0:T(8,128)(2,1)S(1)} copy-done((bf16[1,256,256]{2,1,0:T(8,128)(2,1)S(1)}, bf16[1,256,256]{2,1,0:T(8,128)(2,1)}, u32[]{:S(2)}) %copy-start.3) | copy-done | bytes 131096
  5.5 0.0 copy-start.4
  5.5 0.9 %copy-done.4 = bf16[1,256,256]{2,1,0:T(8,128)(2,1)S(1)} copy-done((bf16[1,256,256]{2,1,0:T(8,128)(2,1)S(1)}, bf16[1,256,256]{2,1,0:T(8,128)(2,1)}, u32[]{:S(2)}) %copy-start.4) | copy-done | bytes 131096
  6.4 0.0 copy-start.5
  6.4 0.8 %copy-done.5 = bf16[1,2,16,1024]{3,2,1,0:T(8,128)(2,1)S(1)} copy-done((bf16[1,2,16,1024]{3,2,1,0:T(8,128)(2,1)S(1)}, bf16[1,2,16,1024]{3,2,1,0:T(8,128)(2,1)}, u32[]{:S(2)}) %copy-start.5) | copy-done | bytes 65560
  7.3 0.0 copy-start.6
  7.3 0.7 %copy-done.6 = s32[1,2,256]{2,1,0:T(2,128)S(1)} copy-done((s32[1,2,256]{2,1,0:T(2,128)S(1)}, s32[1,2,256]{2,1,0:T(2,128)}, u32[]{:S(2)}) %copy-start.6) | copy-done | bytes 2072
  8.0 0.0 copy-start.7
  8.0 0.7 %copy-done.7 = s32[1,2,2,4]{3,2,1,0:T(2,128)S(1)} copy-done((s32[1,2,2,4]{3,2,1,0:T(2,128)S(1)}, s32[1,2,2,4]{3,2,1,0:T(2,128)}, u32[]{:S(2)}) %copy-start.7) | copy-done | bytes 88
  8.6 0.0 copy-start.8
  8.6 0.7 %copy-done.8 = s32[1,2,4]{2,1,0:T(2,128)S(1)} copy-done((s32[1,2,4]{2,1,0:T(2,128)S(1)}, s32[1,2,4]{2,1,0:T(2,128)}, u32[]{:S(2)}) %copy-start.8) | copy-done | bytes 56
  9.3 55.0 %panels_update.1 = bf16[1024,1024]{1,0:T(8,128)(2,1)S(1)} custom-call(bf16[1024,1024]{1,0:T(8,128)(2,1)S(1)} %bitcast.14, bf16[2,16,1024]{2,1,0:T(8,128)(2,1)S(1)} %bitcast.19, bf16[2,16,2048]{2,1,0:T(8,128)(2,1)S(1)} %reshape.3.uh_ref, bf16[2,256,256]{2,1,0:T(8,128)(2,1)S(1)} %bitcast.15, bf16[2,256,256]{2,1,0:T(8,128)(2,1)S(1)} %bitcast.16, ...), custom_call_target="tpu_custom_call" | custom-call | tf_op jit(solution)/shard_map/panels_update/pallas_call | solution.py:284
  64.4 1.3 %copy.13 = bf16[1024,1,1024]{2,0,1:T(8,128)(2,1)} copy(bf16[1024,1,1024]{2,0,1:T(8,128)(2,1)S(1)} %bitcast.13) | data formatting | bytes 4194304
Async XLA Ops:
  1.1 1.6 %copy-start = (bf16[1024,1,1024]{2,0,1:T(8,128)(2,1)S(1)}, bf16[1024,1,1024]{2,0,1:T(8,128)(2,1)}, u32[]{:S(2)}) copy-start(bf16[1024,1,1024]{2,0,1:T(8,128)(2,1)} %param.10) | copy-start | bytes 6291460
  2.7 0.9 %copy-start.1 = (bf16[1,2,256,256]{3,2,1,0:T(8,128)(2,1)S(1)}, bf16[1,2,256,256]{3,2,1,0:T(8,128)(2,1)}, u32[]{:S(2)}) copy-start(bf16[1,2,256,256]{3,2,1,0:T(8,128)(2,1)} %param.13) | copy-start | bytes 786436
  3.7 0.9 %copy-start.2 = (bf16[1,2,256,256]{3,2,1,0:T(8,128)(2,1)S(1)}, bf16[1,2,256,256]{3,2,1,0:T(8,128)(2,1)}, u32[]{:S(2)}) copy-start(bf16[1,2,256,256]{3,2,1,0:T(8,128)(2,1)} %param.14) | copy-start | bytes 786436
  4.6 0.9 %copy-start.3 = (bf16[1,256,256]{2,1,0:T(8,128)(2,1)S(1)}, bf16[1,256,256]{2,1,0:T(8,128)(2,1)}, u32[]{:S(2)}) copy-start(bf16[1,256,256]{2,1,0:T(8,128)(2,1)} %param.15) | copy-start | bytes 393220
  5.5 0.9 %copy-start.4 = (bf16[1,256,256]{2,1,0:T(8,128)(2,1)S(1)}, bf16[1,256,256]{2,1,0:T(8,128)(2,1)}, u32[]{:S(2)}) copy-start(bf16[1,256,256]{2,1,0:T(8,128)(2,1)} %param.16) | copy-start | bytes 393220
  6.4 0.8 %copy-start.5 = (bf16[1,2,16,1024]{3,2,1,0:T(8,128)(2,1)S(1)}, bf16[1,2,16,1024]{3,2,1,0:T(8,128)(2,1)}, u32[]{:S(2)}) copy-start(bf16[1,2,16,1024]{3,2,1,0:T(8,128)(2,1)} %param.11) | copy-start | bytes 196612
  7.3 0.7 %copy-start.6 = (s32[1,2,256]{2,1,0:T(2,128)S(1)}, s32[1,2,256]{2,1,0:T(2,128)}, u32[]{:S(2)}) copy-start(s32[1,2,256]{2,1,0:T(2,128)} %param.17) | copy-start | bytes 6148
  8.0 0.7 %copy-start.7 = (s32[1,2,2,4]{3,2,1,0:T(2,128)S(1)}, s32[1,2,2,4]{3,2,1,0:T(2,128)}, u32[]{:S(2)}) copy-start(s32[1,2,2,4]{3,2,1,0:T(2,128)} %param.19) | copy-start | bytes 196
  8.6 0.7 %copy-start.8 = (s32[1,2,4]{2,1,0:T(2,128)S(1)}, s32[1,2,4]{2,1,0:T(2,128)}, u32[]{:S(2)}) copy-start(s32[1,2,4]{2,1,0:T(2,128)} %param.18) | copy-start | bytes 100

commit v2 on v0

v2 whole, which is shorter than its diff:
```python
import jax
import jax.numpy as jnp
from jax import lax
from jax.experimental import pallas as pl
from jax.experimental.pallas import tpu as pltpu
from jax.sharding import PartitionSpec as P

NZ, NX, NY = 4, 4, 8
NB = 256
SUB = 16
W = 1024
PANEL = 2 * W
CROSS = PANEL + 6 * NB
M0, M1, V, UI0, UI1, WW = (PANEL + i * NB for i in range(6))
COPIES = 128
F32, BF16 = jnp.float32, jnp.bfloat16


def dot(a, b):
    return jnp.dot(a, b, preferred_element_type=F32)


def dot_tn(a, b):
    return lax.dot_general(a, b, (((0,), (0,)), ((), ())), preferred_element_type=F32)


def dot_nt(a, b):
    return lax.dot_general(a, b, (((1,), (1,)), ((), ())), preferred_element_type=F32)


def kernel(trail_ref, *refs):
    body(trail_ref, refs[:9], refs[9], refs[10:19], *refs[19:])


def body(
    trail_ref, sources, out_ref, held,
    lo, xb, stage, uh, ub, own, masks, xmasks, lf, uf, acc, trail_v, out_v,
    send, recv, local,
):
    layer = lax.axis_index("layer")
    row = lax.axis_index("row")
    col = lax.axis_index("col")
    zl, x, y, core = row // NX, row % NX, col // 2, col % 2

    def at(dl=0, dz=0, dx=0, dy=0, k=None, mirror=False, dc=0):
        to_z = NZ - 1 - zl if mirror else (zl + dz + NZ) % NZ
        return (
            (layer + dl) % 2,
            to_z * NX + (x + dx + NX) % NX,
            (y + dy + NY) % NY * 2 + ((core + dc) % 2 if k is None else k),
        )

    def lslot(dy, k=None):
        first = (y + dy + NY) % NY * 2 * SUB
        if k is None:
            return pl.ds(pl.multiple_of(first, 2 * SUB), 2 * SUB)
        return pl.ds(pl.multiple_of(first + k * SUB, SUB), SUB)

    def uslot(i, dz, dx):
        first = i * NB + ((zl + dz + NZ) % NZ * NX + (x + dx + NX) % NX) * SUB
        return pl.ds(pl.multiple_of(first, SUB), SUB)

    barrier = pltpu.get_barrier_semaphore()

    def greet(**to):
        pl.semaphore_signal(barrier, 1, device_id=at(**to), device_id_type=pl.DeviceIdType.MESH)

    greet(dc=1)

    @pl.when(core == 0)
    def _():
        greet(dl=1, k=0)
        for k in range(2):
            greet(dx=1, k=k)
            greet(dx=-1, k=k)
            for j in (1, 2, 3):
                greet(dz=j, k=k)
            greet(dl=1, mirror=True, k=k)

    @pl.when(core == 1)
    def _():
        for k in range(2):
            greet(dy=1, k=k)
            greet(dy=-1, k=k)
            greet(dl=1, k=k)
        greet(dy=2, k=1)
        greet(dy=-2, k=1)

    lp_ref, up_ref, li_ref, ui_ref, above_ref, left_ref, order_ref, rmask_ref, cmask_ref = held
    loads = [
        pltpu.make_async_copy(src, dst, local.at[2 + i])
        for i, (src, dst) in enumerate(zip(sources, held))
    ]
    for copy in loads:
        copy.start()
    fetch = pltpu.make_async_copy(trail_ref, trail_v, local.at[0])
    fetch.start()

    loads[0].wait()
    loads[1].wait()
    for k in range(2):
        stage[:, pl.ds(k * W, W)] = lp_ref[k]
        for h in range(2):
            uh[h, :, pl.ds(k * W, W)] = up_ref[k, :, h, :]
    mine = lslot(0, core)
    lo[mine] = stage[:, :PANEL]
    lanes = pl.ds(pl.multiple_of(core * PANEL, PANEL), PANEL)

    ub[uslot(0, 0, 0), lanes] = uh[layer]
    for copy in loads[2:]:
        copy.wait()
    masks[...] = jnp.zeros_like(masks)
    masks[0:2, 0:4] = rmask_ref[...].astype(F32)
    for k in range(2):
        for h in range(2):
            r = 2 + 2 * h + k
            masks[r : r + 1, 0:4] = cmask_ref[k, h : h + 1, :].astype(F32)

    place = lax.broadcasted_iota(jnp.int32, (NB, NB), 0)

    def permuted(rows, k):
        hot = jnp.where(place == order_ref[k : k + 1, :], 1.0, 0.0).astype(BF16)
        return dot_nt(rows, hot).astype(BF16)

    share = mine
    m0 = permuted(li_ref[0, share], 0)
    m1 = permuted(li_ref[1, share], 1)
    lower_cross = dot(left_ref[...], ui_ref[0]).astype(BF16)
    upper_cross = dot(m0, above_ref[...]).astype(BF16)
    for place_at, value in (
        (M0, m0),
        (M1, m1),
        (V, dot(m1, lower_cross).astype(BF16)),
        (UI0, ui_ref[0, share]),
        (UI1, ui_ref[1, share]),
        (WW, dot(upper_cross, ui_ref[1]).astype(BF16)),
    ):
        stage[:, pl.ds(place_at, NB)] = value

    pl.semaphore_wait(barrier, 11 + core)

    names = {}

    def sem(name):
        return names.setdefault(name, len(names))

    def make(name, src, dst, index=None, **to):
        i = sem(name) if index is None else sem(name) + index
        return pltpu.make_async_remote_copy(
            src_ref=src, dst_ref=dst, send_sem=send.at[i], recv_sem=recv.at[i],
            device_id=at(**to), device_id_type=pl.DeviceIdType.MESH,
        )

    def pair(name):
        i = sem((name, 0))
        assert sem((name, 1)) == i + 1
        return (name, 0)

    def first(name, src, dst, **to):
        copy = make(pair(name), src, dst, index=core, **to)
        copy.start()
        return copy

    own_u, own_l = ub.at[uslot(0, 0, 0), lanes], lo.at[mine]
    begun = [
        first("p00", uh.at[layer], own_u, dx=1, k=0),
        first("m00", uh.at[layer], own_u, dx=-1, k=0),
        first("up1", own_l, own_l, dy=1, k=1),
        first("down1", own_l, own_l, dy=-1, k=1),
        first("z01", uh.at[layer], own_u, dz=1, k=0),
        first("z03", uh.at[layer], own_u, dz=3, k=0),
        first("cross", stage, xb.at[mine], dl=1, k=1),
        first("z02", uh.at[layer], own_u, dz=2, k=0),
        first("mirror", uh.at[1 - layer], ub.at[uslot(1, 0, 0), lanes], dl=1, mirror=True, k=0),
        first("sib", own_l, own_l, dc=1),
        first("masks", masks, xmasks, dl=1),
    ]

    def got(name, dst, k=None):
        index = None if k is None else k
        make(pair(name) if k is not None else name, dst, dst, index=index, dc=1).wait_recv()

    def go(list_, name, ref, **to):
        copy = make(name, ref, ref, **to)
        copy.start()
        list_.append(copy)

    def upper_work(steps):
        sent = []
        a, b = pl.ds(0, PANEL), pl.ds(PANEL, PANEL)

        def row_of(i, j, dx):
            if i == 0:
                return uslot(0, -j, dx)
            holder = (zl - j + NZ) % NZ
            first_row = NB + ((NZ - 1 - holder) * NX + (x + dx + NX) % NX) * SUB
            return pl.ds(pl.multiple_of(first_row, SUB), SUB)

        def spread(i, j):
            rows = row_of(i, j, 0)
            if i == 0:
                got(f"z0{j}", ub.at[rows, a], 0)
                got(f"z0{j}", ub.at[rows, b], 1)
            elif j == 0:
                got("mirror", ub.at[rows, a], 0)
                got("mirror", ub.at[rows, b], 1)
            else:
                got(("z1", j), ub.at[rows])
            go(sent, ("p", i, j), ub.at[rows], dx=1, k=0)
            go(sent, ("m", i, j), ub.at[rows], dx=-1, k=0)
            if i == 1 and j == 0:
                for d in (1, 3, 2):
                    go(sent, ("z1", d), ub.at[rows], dz=d, k=0)

        def forward(i, j):
            left, right = row_of(i, j, -1), row_of(i, j, 1)
            if (i, j) == (0, 0):
                got("p00", ub.at[left, a], 0)
            else:
                got(("p", i, j), ub.at[left])
            go(sent, ("f", i, j), ub.at[left, a], dx=1, k=0)
            if (i, j) == (0, 0):
                got("m00", ub.at[right, b], 1)
            else:
                got(("m", i, j), ub.at[right])
            go(sent, ("g", i, j), ub.at[right, b], dx=-1, k=0)

        def hand(i, j):
            far = row_of(i, j, 2)
            if (i, j) == (0, 0):
                got("p00", ub.at[row_of(0, 0, -1), b], 1)
                got("m00", ub.at[row_of(0, 0, 1), a], 0)
                for dx in (-1, 1):
                    go(sent, ("h", dx), ub.at[row_of(0, 0, dx), b], dc=1)
            got(("f", i, j), ub.at[far, a])
            got(("g", i, j), ub.at[far, b])
            if (i, j) == (0, 0):
                go(sent, ("h", 2), ub.at[far, b], dc=1)
            else:
                go(sent, ("h", i, j), ub.at[quad(i, j), b], dc=1)

        def quad(i, j):
            holder = (zl - j + NZ) % NZ
            base_row = i * NB + (holder if i == 0 else NZ - 1 - holder) * NX * SUB
            return pl.ds(pl.multiple_of(base_row, NX * SUB), NX * SUB)

        def lower_ready(i):
            buf = (lo, xb)[i]
            if i == 0:
                got("sib", lo.at[lslot(0, 1)], 1)
            for d in (0, 1, -1, 2, -2, 3, -3, 4):
                if i == 1 or d != 0:
                    got(("s", i, d), buf.at[lslot(d)])

        steps(spread, forward, hand, lower_ready)
        for copy in sent:
            copy.wait_send()

    def lower_work(steps):
        sent = []

        def pieces(i, s, d):
            buf = (lo, xb)[i]
            for k in range(2):
                rows = lslot(-s * d, k)
                if i == 0 and s == 1:
                    got("up1" if d == 1 else "down1", buf.at[rows], k)
                else:
                    got(("r", i, s, d, k), buf.at[rows])
                go(sent, ("r", i, s + 1, d, k), buf.at[rows], dy=d, k=1)
                if s == 2 and k == (0 if d == 1 else 1):
                    go(sent, ("far", i, d), buf.at[rows], dy=2 * d, k=1)
            go(sent, ("s", i, -s * d), buf.at[lslot(-s * d)], dc=1)

        def cross():
            for k in range(2):
                rows = lslot(0, k)
                got("cross", xb.at[rows], k)
                for d in (1, -1):
                    go(sent, ("r", 1, 1, d, k), xb.at[rows], dy=d, k=1)
            go(sent, ("s", 1, 0), xb.at[lslot(0)], dc=1)

        def step(i, s):
            for d in (1, -1):
                pieces(i, s, d)

        def last(i):
            buf = (lo, xb)[i]
            for d in (1, -1):
                for k in range(2):
                    got(("r", i, 3, d, k), buf.at[lslot(-3 * d, k)])
                go(sent, ("s", i, -3 * d), buf.at[lslot(-3 * d)], dc=1)
            for d, k in ((1, 0), (-1, 1)):
                got(("far", i, d), buf.at[lslot(4, k)])
            go(sent, ("s", i, 4), buf.at[lslot(4)], dc=1)

        def own_ready():
            got("sib", lo.at[lslot(0, 0)], 0)

        def upper_ready(i):
            b = pl.ds(PANEL, PANEL)
            for j in range(NZ):
                if (i, j) == (0, 0):
                    for dx in (-1, 1, 2):
                        got(("h", dx), ub.at[uslot(0, 0, dx), b])
                    continue
                holder = (zl - j + NZ) % NZ
                base_row = i * NB + (holder if i == 0 else NZ - 1 - holder) * NX * SUB
                got(("h", i, j), ub.at[pl.ds(pl.multiple_of(base_row, NX * SUB), NX * SUB), b])

        steps(cross, step, last, own_ready, upper_ready)
        for copy in sent:
            copy.wait_send()

    def own_small():
        own[0] = permuted(li_ref[0], 0)
        own[1] = permuted(li_ref[1], 1)
        own[2] = dot(own[1], lower_cross).astype(BF16)
        own[3] = dot(dot(own[0], above_ref[...]).astype(BF16), ui_ref[1]).astype(BF16)

    def lower_factors(i, b):
        if i == 0:
            buf, ui0, ui1, w, mask = lo, ui_ref[0], ui_ref[1], own[3], masks
        else:
            buf, mask = xb, xmasks
            ui0, ui1, w = (xb[:, pl.ds(c, NB)] for c in (UI0, UI1, WW))
        rows = pl.ds(b * NB, NB)
        first = (dot_tn(buf[:, pl.ds(b * NB, NB)], ui0) * mask[0:1, b : b + 1]).astype(BF16)
        second = dot_tn(buf[:, pl.ds(W + b * NB, NB)], ui1) - dot(first, w)
        lf[i, rows, 0:NB] = first
        lf[i, rows, NB : 2 * NB] = (second * mask[1:2, b : b + 1]).astype(BF16)

    def upper_factors(i, b):
        rows = pl.ds(i * NB, NB)
        if i == 0:
            m0, m1, v, mask = own[0], own[1], own[2], masks
        else:
            mask = xmasks
            m0, m1, v = (xb[:, pl.ds(c, NB)] for c in (M0, M1, V))
        c0 = mask[pl.ds(2 + 2 * layer, 1), :]
        c1 = mask[pl.ds(3 + 2 * layer, 1), :]
        cols = pl.ds(b * NB, NB)
        at0 = pl.ds(pl.multiple_of(core * PANEL + b * NB, NB), NB)
        at1 = pl.ds(pl.multiple_of(core * PANEL + W + b * NB, NB), NB)
        first = (dot(m0, ub[rows, at0]) * c0[:, b : b + 1]).astype(BF16)
        second = dot(m1, ub[rows, at1]) - dot(v, first)
        uf[i, 0:NB, cols] = first
        uf[i, NB : 2 * NB, cols] = (second * c1[:, b : b + 1]).astype(BF16)

    def product(i, b):
        return dot(lf[i, pl.ds(b * NB, NB)], uf[i])

    def base():
        @pl.loop(0, 4)
        def _(b):
            rows = pl.ds(pl.multiple_of(b * NB, NB), NB)
            acc[rows] = product(0, b)

    def finish():
        @pl.loop(0, 4)
        def _(b):
            rows = pl.ds(pl.multiple_of(b * NB, NB), NB)
            total = acc[rows] + product(1, b)
            out_v[rows] = (trail_v[rows].astype(F32) - total).astype(BF16)

    @pl.when(core == 0)
    def _():
        def steps(spread, forward, hand, lower_ready):
            forward(0, 0)
            spread(0, 1)
            spread(0, 3)
            spread(0, 2)
            own_small()
            forward(0, 1)
            spread(1, 0)
            hand(0, 0)
            forward(0, 3)
            forward(0, 2)
            forward(1, 0)
            hand(0, 1)
            spread(1, 1)
            spread(1, 3)
            hand(0, 3)
            spread(1, 2)
            hand(0, 2)
            lower_ready(0)
            for b in range(4):
                lower_factors(0, b)
            forward(1, 1)
            forward(1, 3)
            hand(1, 0)
            forward(1, 2)
            for b in range(4):
                upper_factors(0, b)
            hand(1, 1)
            hand(1, 3)
            hand(1, 2)
            base()
            lower_ready(1)

        upper_work(steps)

    @pl.when(core == 1)
    def _():
        def steps(cross, step, last, own_ready, upper_ready):
            own_ready()
            step(0, 1)
            own_small()
            step(0, 2)
            cross()
            last(0)
            step(1, 1)
            for b in range(4):
                lower_factors(0, b)
            step(1, 2)
            upper_ready(0)
            for b in range(4):
                upper_factors(0, b)
            last(1)
            base()
            upper_ready(1)

        lower_work(steps)

    got("masks", xmasks, core)
    for b in range(4):
        lower_factors(1, b)
    for b in range(4):
        upper_factors(1, b)
    fetch.wait()
    finish()

    put = pltpu.make_async_copy(out_v, out_ref, local.at[1])
    put.start()
    for copy in begun:
        copy.wait_send()
    put.wait()


def on_device(trail, lower, upper, li, ui, above, left, order, rmask, cmask):
    operands = (lower[0], upper[0], li[0], ui[0], above[0], left[0], order[0], rmask[0], cmask[0])
    hbm = pl.BlockSpec(memory_space=pltpu.HBM)
    out = pl.pallas_call(
        kernel,
        out_shape=jax.ShapeDtypeStruct((W, W), BF16),
        in_specs=[hbm] * 10,
        out_specs=pl.BlockSpec(memory_space=pl.ANY),
        scratch_shapes=[pltpu.VMEM(a.shape, a.dtype) for a in operands]
        + [
            pltpu.VMEM((NB, PANEL), BF16),
            pltpu.VMEM((NB, CROSS), BF16),
            pltpu.VMEM((SUB, CROSS), BF16),
            pltpu.VMEM((2, SUB, PANEL), BF16),
            pltpu.VMEM((2 * NB, 2 * PANEL), BF16),
            pltpu.VMEM((4, NB, NB), BF16),
            pltpu.VMEM((8, 128), F32),
            pltpu.VMEM((8, 128), F32),
            pltpu.VMEM((2, W, 2 * NB), BF16),
            pltpu.VMEM((2, 2 * NB, W), BF16),
            pltpu.VMEM((W, W), F32),
            pltpu.VMEM((W, W), BF16),
            pltpu.VMEM((W, W), BF16),
            pltpu.SemaphoreType.DMA((COPIES,)),
            pltpu.SemaphoreType.DMA((COPIES,)),
            pltpu.SemaphoreType.DMA((11,)),
        ],
        compiler_params=pltpu.CompilerParams(
            collective_id=0, has_side_effects=True, vmem_limit_bytes=60 * 2**20
        ),
        name="panels_update",
    )(trail[:, 0, :], *operands)
    return out[:, None, :]


def solution(mesh):
    placed = (
        P("row", "layer", "col"),
        P("layer", None, "col", "row"),
        P("layer", None, "row", None, "col"),
        P("layer", None, None, None),
        P("layer", None, None, None),
        P("layer", None, None),
        P("layer", None, None),
        P("layer", None, None),
        P("layer", None, "row"),
        P("layer", None, None, "col"),
    )
    return jax.shard_map(
        on_device, mesh=mesh, in_specs=placed, out_specs=P("row", "layer", "col"), check_vma=False
    )
```

time: 292 us -> 53.9 us (0.18)
  waiting for transfers between devices: 235 us -> 0 us
  Pallas kernels: 0 us -> 50.7 us
  matrix products: 19.8 us -> 0 us
  between operations: 13.3 us -> 0.01 us
  other arithmetic: 10.4 us -> 0 us
  local copies, waits for them, and re-layouts: 12.9 us -> 3.08 us
    reduce_scatter x1 -> x0, waiting for transfers between devices: 120 us -> none  [on_device(): lax.psum_scatter(partial_value.astype(jnp.bfloat16), 'layer', scatter_dim...]
    all_gather x2 -> x0, waiting for transfers between devices: 114 us -> none  [the longest x1 73.3 us: on_device(): rows_all = lax.all_gather(upper_panels, 'row', axis=2, tiled=True)[0]]
    pallas_call x0 -> x1, Pallas kernels: none -> 50.7 us  [on_device(): pl.pallas_call(kernel, out_shape=jax.ShapeDtypeStruct((W, W), BF16), in_s...]
    dot_general x7 -> x0, matrix products: 19.8 us -> none  [the longest x1 5.95 us: on_device(): jnp.dot(lower_second, upper_second, preferred_element_type=jnp.float32)]
    convert_element_type x4 -> x0, other arithmetic: 7.91 us -> none  [the longest x1 3.87 us: on_device(): return (trail.astype(jnp.float32) + summed).astype(jnp.bfloat16)]
    gather x3 -> x0, local copies, waits for them, and re-layouts: 6.11 us -> none  [the longest x1 2.6 us: build_factors(): jnp.take(rows_flat[0], order[0], axis=0)]
    convert_element_type x1 -> x0, local copies, waits for them, and re-layouts: 4.67 us -> none  [on_device(): partial_value.astype(jnp.bfloat16)]
  transfers between devices with their start and end apart: 3 -> 0, of which waited for: 3 -> 0; matrix products, arithmetic and copies ran while one was open for 4% -> 0% of each run, Pallas kernels for 0% -> 0%
where the time goes in v2:
time: 53.9 us; the launch traced here: 53.8 us
  Pallas kernels  50.7 us (94%)
  local copies, waits for them, and re-layouts  3.08 us (6%)
    pallas_call x1, Pallas kernels, on_device(): pl.pallas_call(kernel, out_shape=jax.ShapeDtypeStruct((W, W), BF16), in_s...  50.7 us
    unnamed x1, local copies, waits for them, and re-layouts  3.08 us

profile of v2, /device:TPU:1, one launch (start us, length us, event | category | flops | bytes accessed | tf_op | source)
XLA Modules:
  0.0 53.8 jit_solution(3687756804551365720)
XLA Ops:
  0.0 50.7 %panels_update.1 = bf16[1024,1024]{1,0:T(8,128)(2,1)} custom-call(bf16[1024,1024]{1,0:T(8,128)(2,1)} %bitcast.12, bf16[2,16,1024]{2,1,0:T(8,128)(2,1)} %bitcast.18, bf16[2,16,2,1024]{3,2,1,0:T(2,128)(2,1)} %bitcast.15, bf16[2,256,256]{2,1,0:T(8,128)(2,1)} %bitcast.13, bf16[2,256,256]{2,1,0:T(8,128)(2,1)} %bitcast.14, bf16[256,256]{1,0:T(8,128)(2,1)} %bitcast.16, ...), custom_call_target="tpu_custom_call" | custom-call | tf_op jit(solution)/shard_map/panels_update/pallas_call | solution.py:443
  50.7 3.1 %copy.12 = bf16[1024,1,1024]{2,0,1:T(8,128)(2,1)} copy(bf16[1024,1,1024]{2,0,1:T(8,128)(2,1)} %bitcast.11) | data formatting | bytes 4194304

commit v3 on v0

v3 whole, which is shorter than its diff:
```python
import jax
import jax.numpy as jnp
from jax import lax
from jax.experimental import pallas as pl
from jax.experimental.pallas import tpu as pltpu
from jax.sharding import PartitionSpec as P

NZ, NX, NY = 8, 4, 8
LZ = NZ // 2
NB = 256
SUB = 16
W = 1024
PANEL = 2 * W
CROSS = PANEL + 6 * NB
M0, M1, V, UI0, UI1, WW = (PANEL + i * NB for i in range(6))
COPIES = 128
DIRECT = (4,)
F32, BF16 = jnp.float32, jnp.bfloat16


def dot(a, b):
    return jnp.dot(a, b, preferred_element_type=F32)


def dot_tn(a, b):
    return lax.dot_general(a, b, (((0,), (0,)), ((), ())), preferred_element_type=F32)


def dot_nt(a, b):
    return lax.dot_general(a, b, (((1,), (1,)), ((), ())), preferred_element_type=F32)


def kernel(trail_ref, *refs):
    body(trail_ref, refs[:9], refs[9], refs[10:19], *refs[19:])


def body(
    trail_ref, sources, out_ref, held,
    lo, xb, stage, uh, uu, own, masks, xmasks, lf, uf, trail_v, out_v,
    send, recv, local,
):
    layer = lax.axis_index("layer")
    row = lax.axis_index("row")
    col = lax.axis_index("col")
    z, x, y, core = layer * LZ + row // NX, row % NX, col // 2, col % 2

    def at(dz=0, dx=0, dy=0, dc=0, k=None):
        to = (z + dz + NZ) % NZ
        return (
            to // LZ,
            to % LZ * NX + (x + dx + NX) % NX,
            (y + dy + NY) % NY * 2 + ((core + dc) % 2 if k is None else k),
        )

    def half_of(dz):
        return (z + dz + NZ) % NZ // LZ

    def lslot(dy, k=None):
        start = (y + dy + NY) % NY * 2 * SUB
        if k is None:
            return pl.ds(pl.multiple_of(start, 2 * SUB), 2 * SUB)
        return pl.ds(pl.multiple_of(start + k * SUB, SUB), SUB)

    def uslot(dz, dx=0):
        at_row = ((z + dz + NZ) % NZ * NX + (x + dx + NX) % NX) * SUB
        return pl.ds(pl.multiple_of(at_row, SUB), SUB)

    lp_ref, up_ref, li_ref, ui_ref, above_ref, left_ref, order_ref, rmask_ref, cmask_ref = held
    loads = [
        pltpu.make_async_copy(src, dst, local.at[2 + i])
        for i, (src, dst) in enumerate(zip(sources, held))
    ]
    for copy in loads:
        copy.start()
    barrier = pltpu.get_barrier_semaphore()

    def greet(**to):
        pl.semaphore_signal(barrier, 1, device_id=at(**to), device_id_type=pl.DeviceIdType.MESH)

    for d in (1, -1):
        greet(dx=d)
        greet(dz=d)
        greet(dz=2 * d)
        greet(dy=d)
        greet(dy=2 * d)
    greet(dc=1)
    greet(dz=4)
    greet(dx=2)

    @pl.when(core == 0)
    def _():
        greet(dy=1, k=1)
        greet(dy=-1, k=1)

    @pl.when(core == 1)
    def _():
        greet(dz=4, k=0)

    fetch = pltpu.make_async_copy(trail_ref, trail_v, local.at[0])
    fetch.start()

    loads[0].wait()
    loads[1].wait()
    for k in range(2):
        stage[:, pl.ds(k * W, W)] = lp_ref[k]
        for h in range(2):
            uh[h, :, pl.ds(k * W, W)] = up_ref[k, :, h, :]
    share = lslot(0, core)
    lo[share] = stage[:, :PANEL]
    uu[layer, uslot(0)] = uh[layer]
    pl.semaphore_wait(barrier, 14 + core)

    names = {}
    begun = []

    def sem(name):
        return names.setdefault(name, len(names))

    def make(name, src, dst, index=None, **to):
        if index is None:
            i = sem(name)
        else:
            i = sem((name, 0))
            assert sem((name, 1)) == i + 1
            i = i + index
        return pltpu.make_async_remote_copy(
            src_ref=src, dst_ref=dst, send_sem=send.at[i], recv_sem=recv.at[i],
            device_id=at(**to), device_id_type=pl.DeviceIdType.MESH,
        )

    def go(sent, name, src, dst=None, **to):
        copy = make(name, src, src if dst is None else dst, **to)
        copy.start()
        sent.append(copy)

    def got(name, dst, index=None):
        make(name, dst, dst, index=index, dc=1).wait_recv()

    def zpart(dz, half, i=None):
        if i is None:
            return uu.at[half, uslot(dz)]
        return uu.at[half, uslot(dz), pl.ds(i * W, W)]

    own_l = lo.at[share]

    go(begun, ("p", 0), zpart(0, layer), dx=1)
    go(begun, ("m", 0), zpart(0, layer), dx=-1)
    for other in (0, 1):
        for d in (1, -1):
            h = (half_of(d) + other) % 2
            go(begun, ("z", d, other), uh.at[h], zpart(0, h), dz=d)
        if other == 0:
            go(begun, "up1", own_l, index=core, dy=1, k=0)
            go(begun, "down1", own_l, index=core, dy=-1, k=0)
    go(begun, "sib", own_l, index=core, dc=1)
    for copy in loads[2:]:
        copy.wait()
    masks[...] = jnp.zeros_like(masks)
    masks[0:2, 0:4] = rmask_ref[...].astype(F32)
    for k in range(2):
        for h in range(2):
            r = 2 + 2 * h + k
            masks[r : r + 1, 0:4] = cmask_ref[k, h : h + 1, :].astype(F32)

    place = lax.broadcasted_iota(jnp.int32, (NB, NB), 0)

    def permuted(rows, k):
        hot = jnp.where(place == order_ref[k : k + 1, :], 1.0, 0.0).astype(BF16)
        return dot_nt(rows, hot).astype(BF16)

    m0 = permuted(li_ref[0, share], 0)
    m1 = permuted(li_ref[1, share], 1)
    lower_cross = dot(left_ref[...], ui_ref[0]).astype(BF16)
    upper_cross = dot(m0, above_ref[...]).astype(BF16)
    for place_at, value in (
        (M0, m0),
        (M1, m1),
        (V, dot(m1, lower_cross).astype(BF16)),
        (UI0, ui_ref[0, share]),
        (UI1, ui_ref[1, share]),
        (WW, dot(upper_cross, ui_ref[1]).astype(BF16)),
    ):
        stage[:, pl.ds(place_at, NB)] = value

    go(begun, "cross", stage, xb.at[share], index=core, dz=4, k=1)
    go(begun, "masks", masks, xmasks, dz=4)

    class Plane:
        def __init__(self, sent):
            self.sent = sent

        def hop2(self):
            for other in (0, 1):
                for d in (1, -1):
                    if other == 0:
                        got(("z", d, 1), zpart(-d, 1 - layer))
                    h = (half_of(d) + other) % 2
                    go(self.sent, ("z", 2 * d, other), zpart(-d, h), dz=d)

        def hop3(self):
            for d in (1, -1):
                got(("z", 2 * d, 1), zpart(-2 * d, 1 - layer))
                go(self.sent, ("z", 3 * d, 0), zpart(-2 * d, half_of(d)), dz=d)
                part = zpart(-2 * d, half_of(2 * d), 0 if d == 1 else 1)
                go(self.sent, ("z", 4 * d, 0), part, dz=2 * d)

        def spread(self, *ds):
            for d in ds:
                if d == 4:
                    got(("z", 4, 0), zpart(-4, layer, 0))
                    got(("z", -4, 0), zpart(4, layer, 1))
                else:
                    got(("z", d, 0), zpart(-d, layer))
                go(self.sent, ("p", d), zpart(-d, layer), dx=1)
                go(self.sent, ("m", d), zpart(-d, layer), dx=-1)
                if d in DIRECT:
                    go(self.sent, ("q", d), zpart(-d, layer), dx=2)

        def forward(self, *ds):
            for d in ds:
                left, right = uslot(-d, -1), uslot(-d, 1)
                got(("p", d), uu.at[layer, left])
                if d not in DIRECT:
                    go(self.sent, ("f", d), uu.at[layer, left, pl.ds(0, W)], dx=1)
                got(("m", d), uu.at[layer, right])
                if d not in DIRECT:
                    go(self.sent, ("g", d), uu.at[layer, right, pl.ds(W, W)], dx=-1)

        def end(self):
            for d in (0, 1, -1, 2, -2, 3, -3, 4):
                if d in DIRECT:
                    got(("q", d), uu.at[layer, uslot(-d, 2)])
                    continue
                got(("f", d), uu.at[layer, uslot(-d, 2), pl.ds(0, W)])
                got(("g", d), uu.at[layer, uslot(-d, 2), pl.ds(W, W)])

    class Ring:
        def __init__(self, sent, i):
            self.sent, self.i, self.buf = sent, i, (lo, xb)[i]

        def hand(self, d):
            go(self.sent, ("s", self.i, d), self.buf.at[lslot(d)], dc=1)

        def cross(self):
            for k in range(2):
                rows = self.buf.at[lslot(0, k)]
                got("cross", rows, k)
                for d in (1, -1):
                    go(self.sent, ("r", 1, 1, d, k), rows, dy=d)
            self.hand(0)

        def step(self, s):
            for k in range(2):
                for d in (1, -1):
                    rows = self.buf.at[lslot(-s * d, k)]
                    if self.i == 0 and s == 1:
                        got("up1" if d == 1 else "down1", rows, k)
                    else:
                        got(("r", self.i, s, d, k), rows)
                    go(self.sent, ("r", self.i, s + 1, d, k), rows, dy=d)
                    if s == 2 and k == (0 if d == 1 else 1):
                        go(self.sent, ("far", self.i, d), rows, dy=2 * d)
            self.hand(-s)
            self.hand(s)

        def last(self):
            for d in (1, -1):
                for k in range(2):
                    got(("r", self.i, 3, d, k), self.buf.at[lslot(-3 * d, k)])
                self.hand(-3 * d)
            for d, k in ((1, 0), (-1, 1)):
                got(("far", self.i, d), self.buf.at[lslot(4, k)])
            self.hand(4)

    def lower_ready(i):
        for d in (0, 1, -1, 2, -2, 3, -3, 4):
            if i == 1 or d != 0:
                got(("s", i, d), (lo, xb)[i].at[lslot(d)])

    def own_small():
        own[0] = permuted(li_ref[0], 0)
        own[1] = permuted(li_ref[1], 1)
        own[2] = dot(own[1], lower_cross).astype(BF16)
        own[3] = dot(dot(own[0], above_ref[...]).astype(BF16), ui_ref[1]).astype(BF16)

    def lower_factors(i, b):
        if i == 0:
            buf, ui0, ui1, w, mask = lo, ui_ref[0], ui_ref[1], own[3], masks
        else:
            buf, mask = xb, xmasks
            ui0, ui1, w = (xb[:, pl.ds(c, NB)] for c in (UI0, UI1, WW))
        rows = pl.ds(b * NB, NB)
        first = (dot_tn(buf[:, pl.ds(b * NB, NB)], ui0) * mask[0:1, b : b + 1]).astype(BF16)
        second = dot_tn(buf[:, pl.ds(W + b * NB, NB)], ui1) - dot(first, w)
        lf[i, rows, 0:NB] = first
        lf[i, rows, NB : 2 * NB] = (second * mask[1:2, b : b + 1]).astype(BF16)

    def upper_factors(i, b):
        rows = pl.ds(pl.multiple_of((layer if i == 0 else 1 - layer) * NB, NB), NB)
        if i == 0:
            m0, m1, v, mask = own[0], own[1], own[2], masks
        else:
            mask = xmasks
            m0, m1, v = (xb[:, pl.ds(c, NB)] for c in (M0, M1, V))
        c0 = mask[pl.ds(2 + 2 * layer, 1), :]
        c1 = mask[pl.ds(3 + 2 * layer, 1), :]
        cols = pl.ds(b * NB, NB)
        first = (dot(m0, uu[layer, rows, cols]) * c0[:, b : b + 1]).astype(BF16)
        second = dot(m1, uu[layer, rows, pl.ds(W + b * NB, NB)]) - dot(v, first)
        uf[i, 0:NB, cols] = first
        uf[i, NB : 2 * NB, cols] = (second * c1[:, b : b + 1]).astype(BF16)

    def product(i, b):
        return dot(lf[i, pl.ds(b * NB, NB)], uf[i])

    def finish():
        @pl.loop(0, 4)
        def _(b):
            rows = pl.ds(pl.multiple_of(b * NB, NB), NB)
            total = product(0, b) + product(1, b)
            out_v[rows] = (trail_v[rows].astype(F32) - total).astype(BF16)
            pltpu.make_async_copy(out_v.at[rows], out_ref.at[rows], local.at[1]).start()

    @pl.when(core == 0)
    def _():
        sent = []
        U, L = Plane(sent), Ring(sent, 0)
        U.forward(0)
        U.spread(1, -1)
        L.step(1)
        U.hop2()
        own_small()
        L.step(2)
        U.forward(1, -1)
        U.spread(2, -2)
        U.hop3()
        U.forward(2, -2)
        L.last()
        got("sib", lo.at[lslot(0, 1)], 1)
        U.spread(3, -3)
        U.spread(4)
        for b in range(4):
            lower_factors(0, b)
        U.forward(3, -3, 4)
        lower_ready(1)
        got("masks", xmasks)
        for b in range(4):
            lower_factors(1, b)
        U.end()
        for copy in sent:
            copy.wait_send()

    @pl.when(core == 1)
    def _():
        sent = []
        U, L = Plane(sent), Ring(sent, 1)
        U.forward(0)
        U.spread(1, -1)
        U.hop2()
        own_small()
        L.cross()
        U.forward(1, -1)
        U.spread(2, -2)
        U.hop3()
        L.step(1)
        U.forward(2, -2)
        got("sib", lo.at[lslot(0, 0)], 0)
        U.spread(3, -3)
        U.spread(4)
        L.step(2)
        lower_ready(0)
        for b in range(4):
            lower_factors(0, b)
        U.forward(3, -3, 4)
        L.last()
        got("masks", xmasks)
        for b in range(4):
            lower_factors(1, b)
        U.end()
        for copy in sent:
            copy.wait_send()

    for b in range(4):
        upper_factors(0, b)
    for b in range(4):
        upper_factors(1, b)
    fetch.wait()
    finish()

    for copy in begun:
        copy.wait_send()
    pltpu.make_async_copy(out_v, out_ref, local.at[1]).wait()


def on_device(trail, lower, upper, li, ui, above, left, order, rmask, cmask):
    operands = (lower[0], upper[0], li[0], ui[0], above[0], left[0], order[0], rmask[0], cmask[0])
    hbm = pl.BlockSpec(memory_space=pltpu.HBM)
    out = pl.pallas_call(
        kernel,
        out_shape=jax.ShapeDtypeStruct((W, W), BF16),
        in_specs=[hbm] * 10,
        out_specs=pl.BlockSpec(memory_space=pl.ANY),
        scratch_shapes=[pltpu.VMEM(a.shape, a.dtype) for a in operands]
        + [
            pltpu.VMEM((NB, PANEL), BF16),
            pltpu.VMEM((NB, CROSS), BF16),
            pltpu.VMEM((SUB, CROSS), BF16),
            pltpu.VMEM((2, SUB, PANEL), BF16),
            pltpu.VMEM((2, 2 * NB, PANEL), BF16),
            pltpu.VMEM((4, NB, NB), BF16),
            pltpu.VMEM((8, 128), F32),
            pltpu.VMEM((8, 128), F32),
            pltpu.VMEM((2, W, 2 * NB), BF16),
            pltpu.VMEM((2, 2 * NB, W), BF16),
            pltpu.VMEM((W, W), BF16),
            pltpu.VMEM((W, W), BF16),
            pltpu.SemaphoreType.DMA((COPIES,)),
            pltpu.SemaphoreType.DMA((COPIES,)),
            pltpu.SemaphoreType.DMA((11,)),
        ],
        compiler_params=pltpu.CompilerParams(
            collective_id=0, has_side_effects=True, vmem_limit_bytes=60 * 2**20
        ),
        name="panels_update",
    )(trail[:, 0, :], *operands)
    return out[:, None, :]


def solution(mesh):
    placed = (
        P("row", "layer", "col"),
        P("layer", None, "col", "row"),
        P("layer", None, "row", None, "col"),
        P("layer", None, None, None),
        P("layer", None, None, None),
        P("layer", None, None),
        P("layer", None, None),
        P("layer", None, None),
        P("layer", None, "row"),
        P("layer", None, None, "col"),
    )
    return jax.shard_map(
        on_device, mesh=mesh, in_specs=placed, out_specs=P("row", "layer", "col"), check_vma=False
    )
```

time: 292 us -> 51.6 us (0.18)
  waiting for transfers between devices: 235 us -> 0 us
  Pallas kernels: 0 us -> 48.4 us
  matrix products: 19.8 us -> 0 us
  between operations: 13.3 us -> 0.01 us
  other arithmetic: 10.4 us -> 0 us
  local copies, waits for them, and re-layouts: 12.9 us -> 3.08 us
    reduce_scatter x1 -> x0, waiting for transfers between devices: 120 us -> none  [on_device(): lax.psum_scatter(partial_value.astype(jnp.bfloat16), 'layer', scatter_dim...]
    all_gather x2 -> x0, waiting for transfers between devices: 114 us -> none  [the longest x1 73.3 us: on_device(): rows_all = lax.all_gather(upper_panels, 'row', axis=2, tiled=True)[0]]
    pallas_call x0 -> x1, Pallas kernels: none -> 48.4 us  [on_device(): pl.pallas_call(kernel, out_shape=jax.ShapeDtypeStruct((W, W), BF16), in_s...]
    dot_general x7 -> x0, matrix products: 19.8 us -> none  [the longest x1 5.95 us: on_device(): jnp.dot(lower_second, upper_second, preferred_element_type=jnp.float32)]
    convert_element_type x4 -> x0, other arithmetic: 7.91 us -> none  [the longest x1 3.87 us: on_device(): return (trail.astype(jnp.float32) + summed).astype(jnp.bfloat16)]
    gather x3 -> x0, local copies, waits for them, and re-layouts: 6.11 us -> none  [the longest x1 2.6 us: build_factors(): jnp.take(rows_flat[0], order[0], axis=0)]
    convert_element_type x1 -> x0, local copies, waits for them, and re-layouts: 4.67 us -> none  [on_device(): partial_value.astype(jnp.bfloat16)]
  transfers between devices with their start and end apart: 3 -> 0, of which waited for: 3 -> 0; matrix products, arithmetic and copies ran while one was open for 4% -> 0% of each run, Pallas kernels for 0% -> 0%
where the time goes in v3:
time: 51.6 us; the launch traced here: 51.5 us
  Pallas kernels  48.4 us (94%)
  local copies, waits for them, and re-layouts  3.08 us (6%)
    pallas_call x1, Pallas kernels, on_device(): pl.pallas_call(kernel, out_shape=jax.ShapeDtypeStruct((W, W), BF16), in_s...  48.4 us
    unnamed x1, local copies, waits for them, and re-layouts  3.08 us

profile of v3, /device:TPU:1, one launch (start us, length us, event | category | flops | bytes accessed | tf_op | source)
XLA Modules:
  0.0 51.5 jit_solution(7846399398046842236)
XLA Ops:
  0.0 48.4 %panels_update.1 = bf16[1024,1024]{1,0:T(8,128)(2,1)} custom-call(bf16[1024,1024]{1,0:T(8,128)(2,1)} %bitcast.12, bf16[2,16,1024]{2,1,0:T(8,128)(2,1)} %bitcast.18, bf16[2,16,2,1024]{3,2,1,0:T(2,128)(2,1)} %bitcast.15, bf16[2,256,256]{2,1,0:T(8,128)(2,1)} %bitcast.13, bf16[2,256,256]{2,1,0:T(8,128)(2,1)} %bitcast.14, bf16[256,256]{1,0:T(8,128)(2,1)} %bitcast.16, ...), custom_call_target="tpu_custom_call" | custom-call | tf_op jit(solution)/shard_map/panels_update/pallas_call | solution.py:398
  48.4 3.1 %copy.12 = bf16[1024,1,1024]{2,0,1:T(8,128)(2,1)} copy(bf16[1024,1,1024]{2,0,1:T(8,128)(2,1)} %bitcast.11) | data formatting | bytes 4194304

commit v4 on v3

--- a/solution.py
+++ b/solution.py
@@ -36,7 +36,7 @@
 
 def body(
     trail_ref, sources, out_ref, held,
-    lo, xb, stage, uh, uu, own, masks, xmasks, lf, uf, trail_v, out_v,
+    lo, xb, stage, uh, uu, own, masks, xmasks, lf, uf, acc, trail_v, out_v,
     send, recv, local,
 ):
     layer = lax.axis_index("layer")
@@ -226,8 +226,8 @@
                 if d not in DIRECT:
                     go(self.sent, ("g", d), uu.at[layer, right, pl.ds(W, W)], dx=-1)
 
-        def end(self):
-            for d in (0, 1, -1, 2, -2, 3, -3, 4):
+        def end(self, *ds):
+            for d in ds:
                 if d in DIRECT:
                     got(("q", d), uu.at[layer, uslot(-d, 2)])
                     continue
@@ -313,11 +313,16 @@
     def product(i, b):
         return dot(lf[i, pl.ds(b * NB, NB)], uf[i])
 
+    def base():
+        @pl.loop(0, 4)
+        def _(b):
+            acc[pl.ds(pl.multiple_of(b * NB, NB), NB)] = product(0, b)
+
     def finish():
         @pl.loop(0, 4)
         def _(b):
             rows = pl.ds(pl.multiple_of(b * NB, NB), NB)
-            total = product(0, b) + product(1, b)
+            total = acc[rows] + product(1, b)
             out_v[rows] = (trail_v[rows].astype(F32) - total).astype(BF16)
             pltpu.make_async_copy(out_v.at[rows], out_ref.at[rows], local.at[1]).start()
 
@@ -342,11 +347,15 @@
         for b in range(4):
             lower_factors(0, b)
         U.forward(3, -3, 4)
+        U.end(0, 1, -1, 2, -2, 3, -3)
+        for b in range(4):
+            upper_factors(0, b)
+        base()
         lower_ready(1)
         got("masks", xmasks)
         for b in range(4):
             lower_factors(1, b)
-        U.end()
+        U.end(4)
         for copy in sent:
             copy.wait_send()
 
@@ -373,15 +382,17 @@
             lower_factors(0, b)
         U.forward(3, -3, 4)
         L.last()
+        U.end(0, 1, -1, 2, -2, 3, -3)
+        for b in range(4):
+            upper_factors(0, b)
+        base()
         got("masks", xmasks)
         for b in range(4):
             lower_factors(1, b)
-        U.end()
+        U.end(4)
         for copy in sent:
             copy.wait_send()
 
-    for b in range(4):
-        upper_factors(0, b)
     for b in range(4):
         upper_factors(1, b)
     fetch.wait()
@@ -412,6 +423,7 @@
             pltpu.VMEM((8, 128), F32),
             pltpu.VMEM((2, W, 2 * NB), BF16),
             pltpu.VMEM((2, 2 * NB, W), BF16),
+            pltpu.VMEM((W, W), F32),
             pltpu.VMEM((W, W), BF16),
             pltpu.VMEM((W, W), BF16),
             pltpu.SemaphoreType.DMA((COPIES,)),

time: 51.6 us -> 52.1 us (level)
  no operation moved by 1% of the time
where the time goes in v4:
time: 52.1 us; the launch traced here: 52 us
  Pallas kernels  48.9 us (94%)
  local copies, waits for them, and re-layouts  3.08 us (6%)
    pallas_call x1, Pallas kernels, on_device(): pl.pallas_call(kernel, out_shape=jax.ShapeDtypeStruct((W, W), BF16), in_s...  48.9 us
    unnamed x1, local copies, waits for them, and re-layouts  3.08 us

profile of v4, /device:TPU:1, one launch (start us, length us, event | category | flops | bytes accessed | tf_op | source)
XLA Modules:
  0.0 52.0 jit_solution(16716353353217941083)
XLA Ops:
  0.0 48.9 %panels_update.1 = bf16[1024,1024]{1,0:T(8,128)(2,1)} custom-call(bf16[1024,1024]{1,0:T(8,128)(2,1)} %bitcast.12, bf16[2,16,1024]{2,1,0:T(8,128)(2,1)} %bitcast.18, bf16[2,16,2,1024]{3,2,1,0:T(2,128)(2,1)} %bitcast.15, bf16[2,256,256]{2,1,0:T(8,128)(2,1)} %bitcast.13, bf16[2,256,256]{2,1,0:T(8,128)(2,1)} %bitcast.14, bf16[256,256]{1,0:T(8,128)(2,1)} %bitcast.16, ...), custom_call_target="tpu_custom_call" | custom-call | tf_op jit(solution)/shard_map/panels_update/pallas_call | solution.py:409
  48.9 3.1 %copy.12 = bf16[1024,1,1024]{2,0,1:T(8,128)(2,1)} copy(bf16[1024,1,1024]{2,0,1:T(8,128)(2,1)} %bitcast.11) | data formatting | bytes 4194304
